TPU v7x, 512 devices: a whole 4x8x8 slice. The times are simulated.
512 devices in a mesh: group: 32 (over z_hi, x, core), mp: 16 (over y, z_lo).
Axes of the slice: x: 4, y: 8, z: 8 (z_hi: 4, z_lo: 2; z = z_hi * 2 + z_lo), core: 2. Of those that a mesh axis runs over, the one named last changes fastest.
Arguments:
- queries: bfloat16 [640, 4096], P('group', 'mp'), may hold values from -6 to 6
- new_kv: bfloat16 [2, 640, 2048], P(None, 'group', 'mp'), may hold values from -6 to 6
- kv_pool: bfloat16 [2, 512, 128, 2048], P(None, 'group', None, 'mp'), may hold values from -6 to 6
- block_table: int32 [32, 16], P('group'), may hold values from 0 to 15, each once within a row
- lengths: int32 [32, 4], replicated, may hold values from 1 to 512, as said below
- mig_slot: int32 [32], replicated, may hold values from 0 to 3
- mig_hop: int32 [1], replicated, may hold values from 1 to 31
- handover: int32 [32], replicated, may hold values from 1 to 3
- out_weight: bfloat16 [4096, 7168], P('mp'), may hold values from -0.75 to 0.75
Outputs:
- attn_out: bfloat16 [640, 7168], P('group', 'mp')
Inputs may be any that keep to these rules, and one draw needn't show every extreme that they name: `block_table`: each group's row orders its 16 cache blocks; request b owns entries b * 4 to (b + 1) * 4 - 1. `lengths`: some request holds exactly 512 tokens. Every group sends one request to group (g + mig_hop) mod 32.
All inputs are finite; a program needn't handle non-finite values.
Results may differ from a plain program's by a relative error of at most 0.013.
Values may be sent and summed in bfloat16 or wider, within the bound.
A program may use at most 64 MiB of HBM per device.

v0:
```python
import jax
import jax.numpy as jnp
from jax import lax
from jax.sharding import PartitionSpec as P

HD = 128
MAXB = 4
STEPS = 4
SLOTS = 4
MAXL = 512


masked_score = -1e30


def from_behind(block, axis, distance):
    devices = range(lax.axis_size(axis))
    route = [((i - distance) % len(devices), i) for i in devices]
    return lax.ppermute(block, axis, route)


def attend(queries, keys, values, visible):
    scores = jnp.einsum(
        "trkqd,rjkd->trkqj", queries, keys, preferred_element_type=jnp.float32
    ) * HD ** (-0.5)
    scores = jnp.where(visible[:, :, None, None, :], scores, masked_score)
    maxima = jnp.max(scores, axis=-1)
    weights = jnp.exp(scores - maxima[..., None]).astype(jnp.bfloat16)
    totals = jnp.sum(weights.astype(jnp.float32), axis=-1)
    weighted = jnp.einsum("trkqj,rjkd->trkqd", weights, values, preferred_element_type=jnp.float32)
    return (maxima, totals, weighted)


def on_device(
    queries, new_kv, kv_pool, block_table, lengths, mig_slot, mig_hop, handover, out_weight
):
    groups = lax.axis_size("group")
    own_group = lax.axis_index("group")
    row_width = kv_pool.shape[3]
    kv_dev = row_width // HD
    head_count = queries.shape[1] // HD
    head_share = head_count // kv_dev
    group_hop = mig_hop[0]
    digits = (groups - 1).bit_length()
    source = (own_group - group_hop) % groups
    my_slot = mig_slot[own_group]
    my_hand = handover[own_group]
    src_slot = mig_slot[source]
    src_hand = handover[source]
    step_ids = jnp.arange(STEPS, dtype=jnp.int32)
    slot_ids = jnp.arange(SLOTS + 1, dtype=jnp.int32)
    positions = jnp.arange(MAXL, dtype=jnp.int32)
    own_table = block_table[0].reshape(SLOTS, MAXB)
    own_cache = kv_pool[:, own_table].reshape(2, SLOTS, MAXL, row_width)
    own_new = new_kv.reshape(2, STEPS, SLOTS + 1, row_width)
    asked = queries.reshape(STEPS, SLOTS + 1, kv_dev, head_share, HD)
    leaving = jnp.concatenate(
        [kv_pool[:, own_table[my_slot]].reshape(2, MAXL, row_width), own_new[:, :, my_slot]], axis=1
    )
    for digit in range(digits):
        shifted = from_behind(leaving, "group", 1 << digit)
        leaving = jnp.where(group_hop // (1 << digit) % 2 == 1, shifted, leaving)
    arrived_cache = leaving[:, :MAXL]
    arrived_new = jnp.where(
        (step_ids < src_hand)[None, :, None], leaving[:, MAXL:], own_new[:, :, SLOTS]
    )
    arrived_len = lengths[source, src_slot]
    first_new = jnp.int32(0)
    cached = jnp.concatenate([own_cache, arrived_cache[:, None]], axis=1)
    fresh_kv = jnp.concatenate([own_new[:, :, :SLOTS], arrived_new[:, :, None]], axis=2).transpose(
        0, 2, 1, 3
    )
    keys_values = jnp.concatenate([cached, fresh_kv], axis=2).reshape(
        2, SLOTS + 1, MAXL + STEPS, kv_dev, HD
    )
    cache_len = jnp.concatenate([lengths[own_group], arrived_len[None]])
    new_from = jnp.where(slot_ids == SLOTS, first_new, 0)
    cache_ok = jnp.broadcast_to(
        (positions[None, :] < cache_len[:, None])[None], (STEPS, SLOTS + 1, MAXL)
    )
    new_ok = (step_ids[None, None, :] <= step_ids[:, None, None]) & (
        step_ids[None, None, :] >= new_from[None, :, None]
    )
    visible = jnp.concatenate([cache_ok, new_ok], axis=-1)
    maxima, totals, weighted = attend(asked, keys_values[0], keys_values[1], visible)
    context = (weighted / totals[..., None]).astype(jnp.bfloat16)
    stays = (slot_ids[None, :] < SLOTS) & ~(
        (slot_ids[None, :] == my_slot) & (step_ids[:, None] >= my_hand)
    )
    arrives = (slot_ids[None, :] == SLOTS) & (step_ids[:, None] >= src_hand)
    active = stays | arrives
    context = jnp.where(
        active[:, :, None, None, None], context, jnp.zeros((), jnp.bfloat16)
    ).reshape(STEPS, SLOTS + 1, head_count * HD)
    pieces = []
    for moment in range(STEPS):
        summand = jnp.dot(context[moment], out_weight, preferred_element_type=jnp.float32)
        pieces.append(lax.psum_scatter(summand, "mp", scatter_dimension=1, tiled=True))
    output = jnp.concatenate(pieces, axis=0)
    return output.astype(jnp.bfloat16)


def solution(mesh):
    in_specs = (
        P("group", "mp"),
        P(None, "group", "mp"),
        P(None, "group", None, "mp"),
        P("group", None),
        P(),
        P(),
        P(),
        P(),
        P("mp", None),
    )
    out_specs = P("group", "mp")
    return jax.shard_map(
        on_device, mesh=mesh, in_specs=in_specs, out_specs=out_specs, check_vma=False
    )
```

profile of v0, /device:TPU:6, one launch (start us, length us, event | category | flops | bytes accessed | tf_op | source)
XLA Modules:
  0.0 492.7 jit_solution(12298806120350669238)
XLA Ops:
  7.3 1.4 fusion.19
  11.9 0.7 reshape_squeeze.6
  12.6 0.7 fusion.18
  13.4 0.6 gather_fusion.1
  14.0 1.9 collective-permute-start
  16.0 0.6 iota_compare_fusion.6
  16.6 0.6 broadcast.204
  17.2 1.3 reduce.17
  18.5 0.1 reshape_squeeze.5
  18.6 3.2 collective-permute-done
  21.8 9.1 %collective-permute-start.1 = (bf16[2,516,128]{2,1,0:T(8,128)(2,1)S(1)}, bf16[2,516,128]{2,1,0:T(8,128)(2,1)S(1)}, u32[]{:S(2)}, u32[]{:S(2)}) collective-permute-start(bf16[2,516,128]{2,1,0:T(8,128)(2,1)S(1)} %broadcast_select_fusion), channel_id=1, source_target_pairs={{480,0},{496,16},{0,32},{16,48},{32,64},{48,80},{64,96},{80,112},{... | collective-permute-start | bytes 792584 | tf_op jit(solution)/shard_map/ppermute | solution.py:19
  31.0 0.7 iota_compare_fusion.5
  31.7 0.1 reshape.263
  31.8 6.9 %collective-permute-done.1 = bf16[2,516,128]{2,1,0:T(8,128)(2,1)S(1)} collective-permute-done((bf16[2,516,128]{2,1,0:T(8,128)(2,1)S(1)}, bf16[2,516,128]{2,1,0:T(8,128)(2,1)S(1)}, u32[]{:S(2)}, u32[]{:S(2)}) %collective-permute-start.1) | collective-permute-done | bytes 264224 | tf_op jit(solution)/shard_map/ppermute | solution.py:19
  38.8 1.9 collective-permute-start.2
  40.7 0.6 iota_compare_fusion.3
  42.6 0.9 dynamic-slice_reduce_fusion
  44.1 1.3 dynamic_slice.31
  45.4 0.1 and_or_fusion
  45.4 3.1 collective-permute-done.2
  48.6 21.6 %collective-permute-start.3 = (bf16[2,516,128]{2,1,0:T(8,128)(2,1)S(1)}, bf16[2,516,128]{2,1,0:T(8,128)(2,1)S(1)}, u32[]{:S(2)}, u32[]{:S(2)}) collective-permute-start(bf16[2,516,128]{2,1,0:T(8,128)(2,1)S(1)} %broadcast_select_fusion.2), channel_id=1, source_target_pairs={{384,0},{400,16},{416,32},{432,48},{448,64},{464,80},{480,96},{496... | collective-permute-start | bytes 792584 | tf_op jit(solution)/shard_map/ppermute | solution.py:19
  70.2 0.7 pad_add_fusion.1
  70.9 0.1 iota_compare_fusion
  71.0 4.7 collective-permute-done.3
  75.7 7.7 %collective-permute-start.4 = (bf16[2,516,128]{2,1,0:T(8,128)(2,1)S(1)}, bf16[2,516,128]{2,1,0:T(8,128)(2,1)S(1)}, u32[]{:S(2)}, u32[]{:S(2)}) collective-permute-start(bf16[2,516,128]{2,1,0:T(8,128)(2,1)S(1)} %broadcast_select_fusion.3), channel_id=1, source_target_pairs={{256,0},{272,16},{288,32},{304,48},{320,64},{336,80},{352,96},{368... | collective-permute-start | bytes 792584 | tf_op jit(solution)/shard_map/ppermute | solution.py:19
  83.5 0.1 copy.29
  83.7 0.7 gather_fusion
  84.4 0.1 copy.30
  84.5 0.7 iota_compare_fusion.2
  85.3 5.6 %collective-permute-done.4 = bf16[2,516,128]{2,1,0:T(8,128)(2,1)S(1)} collective-permute-done((bf16[2,516,128]{2,1,0:T(8,128)(2,1)S(1)}, bf16[2,516,128]{2,1,0:T(8,128)(2,1)S(1)}, u32[]{:S(2)}, u32[]{:S(2)}) %collective-permute-start.4) | collective-permute-done | bytes 264224 | tf_op jit(solution)/shard_map/ppermute | solution.py:19
  91.0 0.1 fusion.15
  91.1 0.1 pad_maximum_fusion
  91.2 0.4 fusion.21
  91.6 0.2 convert_reduce_fusion
  91.8 0.3 fusion.4
  92.2 3.4 convolution_bitcast_fusion
  95.6 5.5 %convolution_bitcast_fusion.3 = f32[7168,5]{1,0:T(8,128)} fusion(bf16[256,7168]{1,0:T(8,128)(2,1)} %param.17, bf16[1,5,2,128]{3,2,1,0:T(2,128)(2,1)S(1)} %bitcast.122), kind=kOutput, calls=%fused_computation.5 | convolution fusion | flops 18350080 | bytes 3815936
  101.2 5.4 %convolution_bitcast_fusion.1 = f32[7168,5]{1,0:T(8,128)} fusion(bf16[256,7168]{1,0:T(8,128)(2,1)} %param.17, bf16[1,5,2,128]{3,2,1,0:T(2,128)(2,1)S(1)} %bitcast.121), kind=kOutput, calls=%fused_computation.3 | convolution fusion | flops 18350080 | bytes 3815936
  106.8 5.5 %convolution_bitcast_fusion.2 = f32[7168,5]{1,0:T(8,128)} fusion(bf16[256,7168]{1,0:T(8,128)(2,1)} %param.17, bf16[1,5,2,128]{3,2,1,0:T(2,128)(2,1)S(1)} %bitcast.120), kind=kOutput, calls=%fused_computation.4 | convolution fusion | flops 18350080 | bytes 3815936
  112.3 86.4 %reduce-scatter.19.cloned.1.call-done = f32[448,5]{1,0:T(8,128)} async-done(((f32[7168,5]{1,0:T(8,128)}), f32[448,5]{1,0:T(8,128)}) %reduce-scatter.19.cloned.1.call-update) | async-done | bytes 8976
  198.7 1.0 copy.46
  199.8 94.5 %reduce-scatter.13.cloned.1.call-done = f32[448,5]{1,0:T(8,128)} async-done(((f32[7168,5]{1,0:T(8,128)}), f32[448,5]{1,0:T(8,128)}) %reduce-scatter.13.cloned.1.call-update) | async-done | bytes 8976
  294.2 1.0 copy.40
  295.3 94.0 %reduce-scatter.17.cloned.1.call-done = f32[448,5]{1,0:T(8,128)} async-done(((f32[7168,5]{1,0:T(8,128)}), f32[448,5]{1,0:T(8,128)}) %reduce-scatter.17.cloned.1.call-update) | async-done | bytes 8976
  389.3 1.0 copy.44
  390.4 94.1 %reduce-scatter.15.cloned.1.call-done = f32[448,5]{1,0:T(8,128)} async-done(((f32[7168,5]{1,0:T(8,128)}), f32[448,5]{1,0:T(8,128)}) %reduce-scatter.15.cloned.1.call-update) | async-done | bytes 8976
  484.5 1.0 copy.42
  485.5 0.6 pad_maximum_fusion.2
  (39 shorter events, 0.7 us)
Async XLA Ops:
  6.5 6.8 %copy-start = (bf16[2,16,128,128]{3,2,1,0:T(8,128)(2,1)S(1)}, bf16[2,16,128,128]{3,2,1,0:T(8,128)(2,1)}, u32[]{:S(2)}) copy-start(bf16[2,16,128,128]{3,2,1,0:T(8,128)(2,1)} %param.11) | copy-start | bytes 3145732
  6.5 77.0 %copy-start.2 = (bf16[2,20,128]{2,0,1:T(2,128)(2,1)S(1)}, bf16[2,20,128]{2,0,1:T(2,128)(2,1)}, u32[]{:S(2)}) copy-start(bf16[2,20,128]{2,0,1:T(2,128)(2,1)} %param.10) | copy-start | bytes 30724
  6.5 77.1 %copy-start.3 = (bf16[20,256]{1,0:T(8,128)(2,1)S(1)}, bf16[20,256]{1,0:T(8,128)(2,1)}, u32[]{:S(2)}) copy-start(bf16[20,256]{1,0:T(8,128)(2,1)} %param.9) | copy-start | bytes 30724
  6.5 192.2 %reduce-scatter.19.cloned.1.call-start = ((), (), s32[]{:S(2)}) async-start(), calls=%async_computation.7 | async-start | bytes 3899392
  14.0 7.7 %collective-permute-start = (bf16[2,516,128]{2,1,0:T(8,128)(2,1)S(1)}, bf16[2,516,128]{2,1,0:T(8,128)(2,1)S(1)}, u32[]{:S(2)}, u32[]{:S(2)}) collective-permute-start(bf16[2,516,128]{2,1,0:T(8,128)(2,1)S(1)} %pad_maximum_fusion.1), channel_id=1, source_target_pairs={{496,0},{0,16},{16,32},{32,48},{48,64},{64,80},{80,96},{96,112},{1... | collective-permute-start | bytes 792584 | tf_op jit(solution)/shard_map/ppermute | solution.py:19
  21.8 16.9 %collective-permute-start.1 = (bf16[2,516,128]{2,1,0:T(8,128)(2,1)S(1)}, bf16[2,516,128]{2,1,0:T(8,128)(2,1)S(1)}, u32[]{:S(2)}, u32[]{:S(2)}) collective-permute-start(bf16[2,516,128]{2,1,0:T(8,128)(2,1)S(1)} %broadcast_select_fusion), channel_id=1, source_target_pairs={{480,0},{496,16},{0,32},{16,48},{32,64},{48,80},{64,96},{80,112},{... | collective-permute-start | bytes 792584 | tf_op jit(solution)/shard_map/ppermute | solution.py:19
  38.8 9.8 %collective-permute-start.2 = (bf16[2,516,128]{2,1,0:T(8,128)(2,1)S(1)}, bf16[2,516,128]{2,1,0:T(8,128)(2,1)S(1)}, u32[]{:S(2)}, u32[]{:S(2)}) collective-permute-start(bf16[2,516,128]{2,1,0:T(8,128)(2,1)S(1)} %broadcast_select_fusion.1), channel_id=1, source_target_pairs={{448,0},{464,16},{480,32},{496,48},{0,64},{16,80},{32,96},{48,112}... | collective-permute-start | bytes 792584 | tf_op jit(solution)/shard_map/ppermute | solution.py:19
  48.6 27.1 %collective-permute-start.3 = (bf16[2,516,128]{2,1,0:T(8,128)(2,1)S(1)}, bf16[2,516,128]{2,1,0:T(8,128)(2,1)S(1)}, u32[]{:S(2)}, u32[]{:S(2)}) collective-permute-start(bf16[2,516,128]{2,1,0:T(8,128)(2,1)S(1)} %broadcast_select_fusion.2), channel_id=1, source_target_pairs={{384,0},{400,16},{416,32},{432,48},{448,64},{464,80},{480,96},{496... | collective-permute-start | bytes 792584 | tf_op jit(solution)/shard_map/ppermute | solution.py:19
  75.7 15.2 %collective-permute-start.4 = (bf16[2,516,128]{2,1,0:T(8,128)(2,1)S(1)}, bf16[2,516,128]{2,1,0:T(8,128)(2,1)S(1)}, u32[]{:S(2)}, u32[]{:S(2)}) collective-permute-start(bf16[2,516,128]{2,1,0:T(8,128)(2,1)S(1)} %broadcast_select_fusion.3), channel_id=1, source_target_pairs={{256,0},{272,16},{288,32},{304,48},{320,64},{336,80},{352,96},{368... | collective-permute-start | bytes 792584 | tf_op jit(solution)/shard_map/ppermute | solution.py:19
  84.5 7.6 %copy-start.1 = (bf16[256,7168]{1,0:T(8,128)(2,1)S(1)}, bf16[256,7168]{1,0:T(8,128)(2,1)}, u32[]{:S(2)}) copy-start(bf16[256,7168]{1,0:T(8,128)(2,1)} %param.17) | copy-start | bytes 11010052
  95.6 198.7 %reduce-scatter.13.cloned.1.call-start = ((), (), s32[]{:S(2)}) async-start(), calls=%async_computation.4 | async-start | bytes 3899392
  101.2 288.1 %reduce-scatter.17.cloned.1.call-start = ((), (), s32[]{:S(2)}) async-start(), calls=%async_computation.6 | async-start | bytes 3899392
  106.7 377.8 %reduce-scatter.15.cloned.1.call-start = ((), (), s32[]{:S(2)}) async-start(), calls=%async_computation.5 | async-start | bytes 3899392
Sparse Core Ops, SparseCore 0:
  95.7 102.9 reduce-scatter.18
  201.6 92.6 reduce-scatter.12
  297.1 92.1 reduce-scatter.16
  392.1 92.3 reduce-scatter.14
where the time goes:
time: 494 us; the launch traced here: 493 us
  waiting for transfers between devices  393 us (80%)
  starting transfers between devices  42.4 us (9%)
  matrix products  20.5 us (4%)
  between operations  19.3 us (4%)
  local copies, waits for them, and re-layouts  11.7 us (2%)
  other arithmetic  6.11 us (1%)
    unnamed x8, waiting for transfers between devices  369 us
    ppermute x5, starting transfers between devices, from_behind(): return lax.ppermute(block, axis, route)  42.2 us
    ppermute x5, waiting for transfers between devices, from_behind(): return lax.ppermute(block, axis, route)  23.6 us
    unnamed x4, matrix products  19.9 us
  transfers between devices with their start and end apart: 9, of which 9 were waited for; matrix products, arithmetic and copies ran while one was open for 6% of the time, Pallas kernels for 0%

commit v1 on v0

v1 whole, which is shorter than its diff:
```python
import functools

import jax
import jax.numpy as jnp
from jax import lax
from jax.experimental import pallas as pl
from jax.experimental.pallas import tpu as pltpu
from jax.sharding import PartitionSpec as P

HD = 128
MAXB = 4
STEPS = 4
SLOTS = 4
MAXL = 512
MASKED = -1e30

Z_HI = 4
XC = 8
YS = 8
PAIR = 896
WIN = 512

ORDER = (4, 3, 5, 2, 6, 1, 7, 0)

BF = jnp.bfloat16
F32 = jnp.float32


def remote(src, dst, send, recv, device):
    return pltpu.make_async_remote_copy(
        src_ref=src, dst_ref=dst, send_sem=send, recv_sem=recv,
        device_id=device, device_id_type=pl.DeviceIdType.MESH,
    )


def kernel(
    table, lengths, mig_slot, mig_hop, handover, q_ref, new_ref, kv_hbm, w_hbm, out_ref,
    qf, nf, kv, w, part, zrecv, ysend, yrecv, msg, a1, a2, st1, b0, b1, b2, st2, outf,
    kv_sem, w_sem, zs, zr, ysem, yr, a1s, a1r, a2s, a2r, b1s, b1r, b2s, b2r,
):
    g = lax.axis_index("group")
    m = lax.axis_index("mp")
    plane, spot = g // XC, g % XC
    y, zl = m // 2, m % 2

    kv_copies = [pltpu.make_async_copy(kv_hbm.at[i], kv.at[i], kv_sem.at[i]) for i in range(2)]
    for copy in kv_copies:
        copy.start()
    chunk_of = [(y + off) % YS for off in ORDER]
    w_copies = []
    for i in range(YS):
        columns = pl.ds(pl.multiple_of(chunk_of[i] * PAIR, 128), PAIR)
        w_copies.append(pltpu.make_async_copy(w_hbm.at[:, columns], w.at[i], w_sem.at[i]))
        w_copies[-1].start()

    plane_peers = [{"group": (plane + k) % Z_HI * XC + spot, "mp": m} for k in range(1, Z_HI)]
    spot_peers = [{"group": plane * XC + (spot + k) % XC, "mp": m} for k in range(1, XC)]
    pair_peer = {"group": g, "mp": y * 2 + 1 - zl}
    y_peers = [{"group": g, "mp": chunk_of[i] * 2 + zl} for i in range(YS - 1)]
    barrier = pltpu.get_barrier_semaphore()
    peers = plane_peers + spot_peers + [pair_peer] + y_peers
    for peer in peers:
        pl.semaphore_signal(barrier, inc=1, device_id=peer, device_id_type=pl.DeviceIdType.MESH)

    qf[0] = q_ref[:, :HD].astype(F32)
    qf[1] = q_ref[:, HD:].astype(F32)
    nf[...] = new_ref[...].astype(F32)
    step_rows = [pl.ds(r, STEPS, stride=SLOTS + 1) for r in range(SLOTS + 1)]

    def own_rows(r):
        return (
            jnp.concatenate([qf[0, step_rows[r], :], qf[1, step_rows[r], :]], axis=0),
            nf[0, step_rows[r], :],
            nf[1, step_rows[r], :],
        )

    q4, k4, v4 = own_rows(SLOTS)
    packed = jnp.concatenate([q4, k4, v4], axis=0).astype(BF)
    msg[...] = packed
    a1[0] = packed

    pl.semaphore_wait(barrier, len(peers))

    hop = mig_hop[0]

    def exchange(first, stage1, stage, stage2, s1, r1, s2, r2, towards):
        one = [
            remote(first, stage1.at[k], s1.at[k], r1.at[k], plane_peers[k - 1])
            for k in range(1, Z_HI)
        ]
        for copy in one:
            copy.start()
        for copy in one:
            copy.wait()
        two = []
        for k in range(XC):
            target = plane * XC + (spot + k) % XC
            owner = (target - towards + 64) % 32
            slot = (plane - owner // XC + Z_HI) % Z_HI
            if k == 0:
                stage2[0] = stage1[slot]
            else:
                stage[k] = stage1[slot]
                two.append(remote(stage.at[k], stage2.at[k], s2.at[k], r2.at[k], spot_peers[k - 1]))
                two[-1].start()
        for copy in two:
            copy.wait()
        owner = (g - towards + 64) % 32
        return stage2[(spot - owner % XC + XC) % XC]

    arrived = exchange(msg, a1, st1, a2, a1s, a1r, a2s, a2r, -hop).astype(F32)

    my_slot = mig_slot[g]
    my_hand = handover[g]
    source = (g - hop + 32) % 32
    src_hand = handover[source]

    for copy in kv_copies:
        copy.wait()

    row8 = lax.broadcasted_iota(jnp.int32, (8, 1), 0) % STEPS
    row4 = lax.broadcasted_iota(jnp.int32, (4, 1), 0)
    queries, keys_new, values_new = [], [], []
    for r in range(SLOTS):
        q, k, v = own_rows(r)
        moved = jnp.where(my_slot == r, my_hand, STEPS)
        queries.append(jnp.where(row8 >= moved, arrived[0:8], q).astype(BF))
        keys_new.append(jnp.where(row4 >= moved, arrived[8:12], k))
        values_new.append(jnp.where(row4 >= moved, arrived[12:16], v))
    keys_new = jnp.concatenate(keys_new, axis=0).astype(BF)
    values_new = jnp.concatenate(values_new, axis=0).astype(BF)

    scale = HD ** (-0.5)
    contract_last = (((1,), (1,)), ((), ()))
    lane = lax.broadcasted_iota(jnp.int32, (8, MAXL), 1)
    lane16 = lax.broadcasted_iota(jnp.int32, (8, 16), 1)
    row16 = lax.broadcasted_iota(jnp.int32, (8, 16), 0) % STEPS
    context = []
    for r in range(SLOTS):
        blocks = [table[0, r * MAXB + j] for j in range(MAXB)]
        keys = jnp.concatenate([kv[0, block] for block in blocks], axis=0)
        values = jnp.concatenate([kv[1, block] for block in blocks], axis=0)
        cached = lax.dot_general(queries[r], keys, contract_last, preferred_element_type=F32) * scale
        fresh = lax.dot_general(queries[r], keys_new, contract_last, preferred_element_type=F32) * scale
        cached = jnp.where(lane < lengths[g, r], cached, MASKED)
        fresh = jnp.where((lane16 // STEPS == r) & (lane16 % STEPS <= row16), fresh, MASKED)
        top = jnp.maximum(
            jnp.max(cached, axis=1, keepdims=True), jnp.max(fresh, axis=1, keepdims=True)
        )
        cached = jnp.exp(cached - top).astype(BF)
        fresh = jnp.exp(fresh - top).astype(BF)
        total = jnp.sum(cached.astype(F32), axis=1, keepdims=True) + jnp.sum(
            fresh.astype(F32), axis=1, keepdims=True
        )
        weighted = jnp.dot(cached, values, preferred_element_type=F32) + jnp.dot(
            fresh, values_new, preferred_element_type=F32
        )
        rows = weighted / total
        context.append(jnp.concatenate([rows[:STEPS], rows[STEPS:]], axis=1))
    context = jnp.concatenate(context, axis=0).astype(BF)

    z_copies = []
    theirs = pl.ds(pl.multiple_of((1 - zl) * (PAIR - WIN), 128), WIN)
    ours = pl.ds(pl.multiple_of(zl * (PAIR - WIN), 128), WIN)
    for i in range(YS):
        w_copies[i].wait()
        part[i] = jnp.dot(context, w[i], preferred_element_type=F32).astype(BF)
        z_copies.append(remote(part.at[i, :, theirs], zrecv.at[i], zs.at[i], zr.at[i], pair_peer))
        z_copies[-1].start()

    y_copies = []
    for i in range(YS):
        z_copies[i].wait_recv()
        both = part[i, :, ours].astype(F32) + zrecv[i].astype(F32)
        if i < YS - 1:
            ysend[i] = both.astype(BF)
            y_copies.append(remote(ysend.at[i], yrecv.at[i], ysem.at[i], yr.at[i], y_peers[i]))
            y_copies[-1].start()
    total = both
    for i in range(YS - 1):
        y_copies[i].wait_recv()
        total = total + yrecv[i].astype(F32)
    for copy in z_copies + y_copies:
        copy.wait_send()

    total = jnp.where(zl == 0, total, pltpu.roll(total, PAIR // 2, 1))

    moving = total[0:4]
    for r in range(1, SLOTS):
        moving = jnp.where(my_slot == r, total[4 * r : 4 * r + 4], moving)
    packed = jnp.concatenate([moving[:, c * 128 : c * 128 + 128] for c in range(4)], axis=0).astype(BF)
    b0[...] = packed
    b1[0] = packed
    back = exchange(b0, b1, st2, b2, b1s, b1r, b2s, b2r, hop).astype(F32)
    for c in range(4):
        for r in range(SLOTS):
            moved = jnp.where(my_slot == r, my_hand, STEPS)
            stayed = total[4 * r : 4 * r + 4, c * 128 : c * 128 + 128]
            outf[c, step_rows[r], :] = jnp.where(row4 >= moved, 0.0, stayed)
        outf[c, step_rows[SLOTS], :] = jnp.where(row4 >= src_hand, back[4 * c : 4 * c + 4], 0.0)
    wide = jnp.concatenate([outf[c] for c in range(4)], axis=1)
    out_ref[...] = wide[:, : PAIR // 2].astype(BF)


def on_device(
    queries, new_kv, kv_pool, block_table, lengths, mig_slot, mig_hop, handover, out_weight
):
    rows = STEPS * (SLOTS + 1)
    width = out_weight.shape[1]
    smem = pl.BlockSpec(memory_space=pltpu.SMEM)
    vmem = pl.BlockSpec(memory_space=pltpu.VMEM)
    hbm = pl.BlockSpec(memory_space=pltpu.HBM)
    dma = lambda n: pltpu.SemaphoreType.DMA((n,))
    tile = (16, 128)
    return pl.pallas_call(
        kernel,
        out_shape=jax.ShapeDtypeStruct((rows, PAIR // 2), BF),
        in_specs=[smem] * 5 + [vmem, vmem, hbm, hbm],
        out_specs=vmem,
        scratch_shapes=[
            pltpu.VMEM((2, rows, HD), F32),
            pltpu.VMEM((2, rows, HD), F32),
            pltpu.VMEM(kv_pool.shape, BF),
            pltpu.VMEM((YS, 2 * HD, PAIR), BF),
            pltpu.VMEM((YS, 16, PAIR), BF),
            pltpu.VMEM((YS, 16, WIN), BF),
            pltpu.VMEM((YS, 16, WIN), BF),
            pltpu.VMEM((YS, 16, WIN), BF),
            pltpu.VMEM(tile, BF),
            pltpu.VMEM((Z_HI,) + tile, BF),
            pltpu.VMEM((XC,) + tile, BF),
            pltpu.VMEM((XC,) + tile, BF),
            pltpu.VMEM(tile, BF),
            pltpu.VMEM((Z_HI,) + tile, BF),
            pltpu.VMEM((XC,) + tile, BF),
            pltpu.VMEM((XC,) + tile, BF),
            pltpu.VMEM((4, rows, 128), F32),
            dma(2), dma(YS), dma(YS), dma(YS), dma(YS), dma(YS),
            dma(Z_HI), dma(Z_HI), dma(XC), dma(XC),
            dma(Z_HI), dma(Z_HI), dma(XC), dma(XC),
        ],
        compiler_params=pltpu.CompilerParams(
            collective_id=0, has_side_effects=True, vmem_limit_bytes=32 * 1024 * 1024
        ),
        cost_estimate=pl.CostEstimate(
            flops=2 * 16 * 256 * width, bytes_accessed=5 * 1024 * 1024, transcendentals=32 * 512
        ),
    )(block_table, lengths, mig_slot, mig_hop, handover, queries, new_kv, kv_pool, out_weight)


def solution(mesh):
    in_specs = (
        P("group", "mp"),
        P(None, "group", "mp"),
        P(None, "group", None, "mp"),
        P("group", None),
        P(),
        P(),
        P(),
        P(),
        P("mp", None),
    )
    return jax.shard_map(
        on_device, mesh=mesh, in_specs=in_specs, out_specs=P("group", "mp"), check_vma=False
    )
```

time: 494 us -> 51.4 us (0.10)
  the two profiles are of different devices: /device:TPU:6 before, /device:TPU:1 now
where the time goes in v1:
time: 51.4 us; the launch traced here: 51 us
  Pallas kernels  42.3 us (82%)
  local copies, waits for them, and re-layouts  8.01 us (16%)
  between operations  0.67 us (1%)
    pallas_call x1, Pallas kernels, on_device(): pl.pallas_call(kernel, out_shape=jax.ShapeDtypeStruct((rows, PAIR // 2),...  42.3 us
    unnamed x15, local copies, waits for them, and re-layouts  8.01 us

profile of v1, /device:TPU:1, one launch (start us, length us, event | category | flops | bytes accessed | tf_op | source)
XLA Modules:
  0.0 51.0 jit_solution(8781458888232669353)
XLA Ops:
  0.7 0.7 %copy.11.new_ref = bf16[2,20,128]{2,1,0:T(8,128)(2,1)S(1)} copy(bf16[2,20,128]{2,0,1:T(2,128)(2,1)} %param.10) | data formatting | bytes 20480 | tf_op args[1]
  1.4 0.8 %copy.10.lengths = s32[32,4]{1,0:T(8,128)S(1)} copy(s32[32,4]{0,1:T(4,128)} %param.13) | data formatting | bytes 1024 | tf_op args[4]
  2.1 0.0 copy-start
  2.1 2.0 %copy-done = bf16[256,7168]{1,0:T(8,128)(2,1)S(1)} copy-done((bf16[256,7168]{1,0:T(8,128)(2,1)S(1)}, bf16[256,7168]{1,0:T(8,128)(2,1)}, u32[]{:S(2)}) %copy-start) | copy-done | bytes 3670040
  4.2 0.0 copy-start.1
  4.2 1.2 %copy-done.1 = bf16[2,16,128,128]{3,2,1,0:T(8,128)(2,1)S(1)} copy-done((bf16[2,16,128,128]{3,2,1,0:T(8,128)(2,1)S(1)}, bf16[2,16,128,128]{3,2,1,0:T(8,128)(2,1)}, u32[]{:S(2)}) %copy-start.1) | copy-done | bytes 1048600
  5.4 0.0 copy-start.2
  5.4 0.7 %copy-done.2 = bf16[20,256]{1,0:T(8,128)(2,1)S(1)} copy-done((bf16[20,256]{1,0:T(8,128)(2,1)S(1)}, bf16[20,256]{1,0:T(8,128)(2,1)}, u32[]{:S(2)}) %copy-start.2) | copy-done | bytes 10264
  6.1 0.0 copy-start.3
  6.1 0.7 %copy-done.3 = s32[1,16]{1,0:T(1,128)S(1)} copy-done((s32[1,16]{1,0:T(1,128)S(1)}, s32[1,16]{1,0:T(1,128)}, u32[]{:S(2)}) %copy-start.3) | copy-done | bytes 88
  6.7 0.0 copy-start.4
  6.8 0.7 %copy-done.4 = s32[32]{0:T(128)S(1)} copy-done((s32[32]{0:T(128)S(1)}, s32[32]{0:T(128)}, u32[]{:S(2)}) %copy-start.4) | copy-done | bytes 152
  7.4 0.0 copy-start.5
  7.4 0.7 %copy-done.5 = s32[32]{0:T(128)S(1)} copy-done((s32[32]{0:T(128)S(1)}, s32[32]{0:T(128)}, u32[]{:S(2)}) %copy-start.5) | copy-done | bytes 152
  8.1 42.3 %shard_map.91 = bf16[20,448]{1,0:T(8,128)(2,1)S(1)} custom-call(s32[1,16]{1,0:T(1,128)S(1)} %copy-done.3, s32[32,4]{1,0:T(8,128)S(1)} %copy.10.lengths, s32[32]{0:T(128)S(1)} %copy-done.4, s32[1]{0:T(128)S(6)} %copy.13.mig_hop, s32[32]{0:T(128)S(1)} %copy-done.5, bf16[20,256]{1,0:T(8,128)(2,1)S(1)} %copy-done.2, bf16[2,20,128]{2,1,0:T(8,128)(2,1)S(1)} %copy.11.new_ref, ...), custom_call_target="tpu_custom_call" | custom-call | flops 58720256 | bytes 5242880 | tf_op jit(solution)/shard_map/pallas_call | solution.py:215
  50.4 0.6 %copy.14 = bf16[20,448]{1,0:T(8,128)(2,1)} copy(bf16[20,448]{1,0:T(8,128)(2,1)S(1)} %shard_map.91) | data formatting | bytes 35840
Async XLA Ops:
  2.1 2.0 %copy-start = (bf16[256,7168]{1,0:T(8,128)(2,1)S(1)}, bf16[256,7168]{1,0:T(8,128)(2,1)}, u32[]{:S(2)}) copy-start(bf16[256,7168]{1,0:T(8,128)(2,1)} %w_hbm.1) | copy-start | bytes 11010052
  4.2 1.2 %copy-start.1 = (bf16[2,16,128,128]{3,2,1,0:T(8,128)(2,1)S(1)}, bf16[2,16,128,128]{3,2,1,0:T(8,128)(2,1)}, u32[]{:S(2)}) copy-start(bf16[2,16,128,128]{3,2,1,0:T(8,128)(2,1)} %kv_hbm.1) | copy-start | bytes 3145732
  5.4 0.7 %copy-start.2 = (bf16[20,256]{1,0:T(8,128)(2,1)S(1)}, bf16[20,256]{1,0:T(8,128)(2,1)}, u32[]{:S(2)}) copy-start(bf16[20,256]{1,0:T(8,128)(2,1)} %q_ref.1) | copy-start | bytes 30724
  6.1 0.7 %copy-start.3 = (s32[1,16]{1,0:T(1,128)S(1)}, s32[1,16]{1,0:T(1,128)}, u32[]{:S(2)}) copy-start(s32[1,16]{1,0:T(1,128)} %table.1) | copy-start | bytes 196
  6.7 0.7 %copy-start.4 = (s32[32]{0:T(128)S(1)}, s32[32]{0:T(128)}, u32[]{:S(2)}) copy-start(s32[32]{0:T(128)} %mig_slot.1) | copy-start | bytes 388
  7.4 0.7 %copy-start.5 = (s32[32]{0:T(128)S(1)}, s32[32]{0:T(128)}, u32[]{:S(2)}) copy-start(s32[32]{0:T(128)} %handover.1) | copy-start | bytes 388

commit v2 on v1

--- a/solution.py
+++ b/solution.py
@@ -14,8 +14,6 @@
 MAXL = 512
 MASKED = -1e30
 
-Z_HI = 4
-XC = 8
 YS = 8
 PAIR = 896
 WIN = 512
@@ -34,15 +32,22 @@
 
 
 def kernel(
-    table, lengths, mig_slot, mig_hop, handover, q_ref, new_ref, kv_hbm, w_hbm, out_ref,
-    qf, nf, kv, w, part, zrecv, ysend, yrecv, msg, a1, a2, st1, b0, b1, b2, st2, outf,
-    kv_sem, w_sem, zs, zr, ysem, yr, a1s, a1r, a2s, a2r, b1s, b1r, b2s, b2r,
+    hop, table_hbm, lengths_hbm, mig_slot_hbm, handover_hbm, q_hbm, new_hbm, kv_hbm, w_hbm,
+    out_ref,
+    table, lengths, mig_slot, handover, q_ref, new_ref, qf, nf, kv, w, part, zrecv, ysend, yrecv, msg, asked, b0, answered, outf,
+    small_sem, kv_sem, w_sem, zs, zr, ysem, yr, move_sem,
 ):
     g = lax.axis_index("group")
     m = lax.axis_index("mp")
-    plane, spot = g // XC, g % XC
     y, zl = m // 2, m % 2
 
+    small = (
+        (q_hbm, q_ref), (new_hbm, new_ref), (mig_slot_hbm, mig_slot), (handover_hbm, handover),
+        (table_hbm, table), (lengths_hbm, lengths),
+    )
+    small = [pltpu.make_async_copy(src, dst, small_sem.at[i]) for i, (src, dst) in enumerate(small)]
+    for copy in small:
+        copy.start()
     kv_copies = [pltpu.make_async_copy(kv_hbm.at[i], kv.at[i], kv_sem.at[i]) for i in range(2)]
     for copy in kv_copies:
         copy.start()
@@ -53,18 +58,19 @@
         w_copies.append(pltpu.make_async_copy(w_hbm.at[:, columns], w.at[i], w_sem.at[i]))
         w_copies[-1].start()
 
-    plane_peers = [{"group": (plane + k) % Z_HI * XC + spot, "mp": m} for k in range(1, Z_HI)]
-    spot_peers = [{"group": plane * XC + (spot + k) % XC, "mp": m} for k in range(1, XC)]
     pair_peer = {"group": g, "mp": y * 2 + 1 - zl}
     y_peers = [{"group": g, "mp": chunk_of[i] * 2 + zl} for i in range(YS - 1)]
     barrier = pltpu.get_barrier_semaphore()
-    peers = plane_peers + spot_peers + [pair_peer] + y_peers
+    peers = y_peers + [pair_peer] + [{"group": (g + k) % 32, "mp": m} for k in (hop, 32 - hop)]
     for peer in peers:
         pl.semaphore_signal(barrier, inc=1, device_id=peer, device_id_type=pl.DeviceIdType.MESH)
 
+    small[0].wait()
+    small[1].wait()
     qf[0] = q_ref[:, :HD].astype(F32)
     qf[1] = q_ref[:, HD:].astype(F32)
-    nf[...] = new_ref[...].astype(F32)
+    nf[0] = new_ref[:, 0, :].astype(F32)
+    nf[1] = new_ref[:, 1, :].astype(F32)
     step_rows = [pl.ds(r, STEPS, stride=SLOTS + 1) for r in range(SLOTS + 1)]
 
     def own_rows(r):
@@ -77,38 +83,16 @@
     q4, k4, v4 = own_rows(SLOTS)
     packed = jnp.concatenate([q4, k4, v4], axis=0).astype(BF)
     msg[...] = packed
-    a1[0] = packed
 
     pl.semaphore_wait(barrier, len(peers))
 
-    hop = mig_hop[0]
-
-    def exchange(first, stage1, stage, stage2, s1, r1, s2, r2, towards):
-        one = [
-            remote(first, stage1.at[k], s1.at[k], r1.at[k], plane_peers[k - 1])
-            for k in range(1, Z_HI)
-        ]
-        for copy in one:
-            copy.start()
-        for copy in one:
-            copy.wait()
-        two = []
-        for k in range(XC):
-            target = plane * XC + (spot + k) % XC
-            owner = (target - towards + 64) % 32
-            slot = (plane - owner // XC + Z_HI) % Z_HI
-            if k == 0:
-                stage2[0] = stage1[slot]
-            else:
-                stage[k] = stage1[slot]
-                two.append(remote(stage.at[k], stage2.at[k], s2.at[k], r2.at[k], spot_peers[k - 1]))
-                two[-1].start()
-        for copy in two:
-            copy.wait()
-        owner = (g - towards + 64) % 32
-        return stage2[(spot - owner % XC + XC) % XC]
-
-    arrived = exchange(msg, a1, st1, a2, a1s, a1r, a2s, a2r, -hop).astype(F32)
+    for copy in small[2:]:
+        copy.wait()
+
+    ask = remote(msg, asked, move_sem.at[0], move_sem.at[1], {"group": (g + 32 - hop) % 32, "mp": m})
+    ask.start()
+    ask.wait_recv()
+    arrived = asked[...].astype(F32)
 
     my_slot = mig_slot[g]
     my_hand = handover[g]
@@ -142,7 +126,7 @@
         values = jnp.concatenate([kv[1, block] for block in blocks], axis=0)
         cached = lax.dot_general(queries[r], keys, contract_last, preferred_element_type=F32) * scale
         fresh = lax.dot_general(queries[r], keys_new, contract_last, preferred_element_type=F32) * scale
-        cached = jnp.where(lane < lengths[g, r], cached, MASKED)
+        cached = jnp.where(lane < lengths[r, g], cached, MASKED)
         fresh = jnp.where((lane16 // STEPS == r) & (lane16 % STEPS <= row16), fresh, MASKED)
         top = jnp.maximum(
             jnp.max(cached, axis=1, keepdims=True), jnp.max(fresh, axis=1, keepdims=True)
@@ -180,7 +164,7 @@
     for i in range(YS - 1):
         y_copies[i].wait_recv()
         total = total + yrecv[i].astype(F32)
-    for copy in z_copies + y_copies:
+    for copy in z_copies + y_copies + [ask]:
         copy.wait_send()
 
     total = jnp.where(zl == 0, total, pltpu.roll(total, PAIR // 2, 1))
@@ -190,8 +174,10 @@
         moving = jnp.where(my_slot == r, total[4 * r : 4 * r + 4], moving)
     packed = jnp.concatenate([moving[:, c * 128 : c * 128 + 128] for c in range(4)], axis=0).astype(BF)
     b0[...] = packed
-    b1[0] = packed
-    back = exchange(b0, b1, st2, b2, b1s, b1r, b2s, b2r, hop).astype(F32)
+    answer = remote(b0, answered, move_sem.at[2], move_sem.at[3], {"group": (g + hop) % 32, "mp": m})
+    answer.start()
+    answer.wait_recv()
+    back = answered[...].astype(F32)
     for c in range(4):
         for r in range(SLOTS):
             moved = jnp.where(my_slot == r, my_hand, STEPS)
@@ -199,6 +185,7 @@
             outf[c, step_rows[r], :] = jnp.where(row4 >= moved, 0.0, stayed)
         outf[c, step_rows[SLOTS], :] = jnp.where(row4 >= src_hand, back[4 * c : 4 * c + 4], 0.0)
     wide = jnp.concatenate([outf[c] for c in range(4)], axis=1)
+    answer.wait_send()
     out_ref[...] = wide[:, : PAIR // 2].astype(BF)
 
 
@@ -207,17 +194,24 @@
 ):
     rows = STEPS * (SLOTS + 1)
     width = out_weight.shape[1]
-    smem = pl.BlockSpec(memory_space=pltpu.SMEM)
+    new_kv = new_kv.transpose(1, 0, 2)
+    lengths = lengths.T
     vmem = pl.BlockSpec(memory_space=pltpu.VMEM)
     hbm = pl.BlockSpec(memory_space=pltpu.HBM)
     dma = lambda n: pltpu.SemaphoreType.DMA((n,))
     tile = (16, 128)
-    return pl.pallas_call(
-        kernel,
+    call = lambda hop: pl.pallas_call(
+        functools.partial(kernel, hop),
         out_shape=jax.ShapeDtypeStruct((rows, PAIR // 2), BF),
-        in_specs=[smem] * 5 + [vmem, vmem, hbm, hbm],
+        in_specs=[hbm] * 8,
         out_specs=vmem,
         scratch_shapes=[
+            pltpu.SMEM(block_table.shape, jnp.int32),
+            pltpu.SMEM(lengths.shape, jnp.int32),
+            pltpu.SMEM(mig_slot.shape, jnp.int32),
+            pltpu.SMEM(handover.shape, jnp.int32),
+            pltpu.VMEM(queries.shape, BF),
+            pltpu.VMEM(new_kv.shape, BF),
             pltpu.VMEM((2, rows, HD), F32),
             pltpu.VMEM((2, rows, HD), F32),
             pltpu.VMEM(kv_pool.shape, BF),
@@ -227,25 +221,24 @@
             pltpu.VMEM((YS, 16, WIN), BF),
             pltpu.VMEM((YS, 16, WIN), BF),
             pltpu.VMEM(tile, BF),
-            pltpu.VMEM((Z_HI,) + tile, BF),
-            pltpu.VMEM((XC,) + tile, BF),
-            pltpu.VMEM((XC,) + tile, BF),
-            pltpu.VMEM(tile, BF),
-            pltpu.VMEM((Z_HI,) + tile, BF),
-            pltpu.VMEM((XC,) + tile, BF),
-            pltpu.VMEM((XC,) + tile, BF),
+            pltpu.VMEM(tile, BF),
+            pltpu.VMEM(tile, BF),
+            pltpu.VMEM(tile, BF),
             pltpu.VMEM((4, rows, 128), F32),
-            dma(2), dma(YS), dma(YS), dma(YS), dma(YS), dma(YS),
-            dma(Z_HI), dma(Z_HI), dma(XC), dma(XC),
-            dma(Z_HI), dma(Z_HI), dma(XC), dma(XC),
+            dma(6), dma(2), dma(YS), dma(YS), dma(YS), dma(YS), dma(YS),
+            dma(4),
         ],
         compiler_params=pltpu.CompilerParams(
-            collective_id=0, has_side_effects=True, vmem_limit_bytes=32 * 1024 * 1024
+            collective_id=hop, has_side_effects=True, vmem_limit_bytes=60 * 1024 * 1024
         ),
         cost_estimate=pl.CostEstimate(
             flops=2 * 16 * 256 * width, bytes_accessed=5 * 1024 * 1024, transcendentals=32 * 512
         ),
-    )(block_table, lengths, mig_slot, mig_hop, handover, queries, new_kv, kv_pool, out_weight)
+    )
+    return lax.switch(
+        mig_hop[0] - 1, [call(hop) for hop in range(1, 32)],
+        block_table, lengths, mig_slot, handover, queries, new_kv, kv_pool, out_weight,
+    )
 
 
 def solution(mesh):

time: 51.4 us -> 33.9 us (0.66)
  the two profiles are of different devices: /device:TPU:1 before, /device:TPU:6 now
where the time goes in v2:
time: 33.9 us; the launch traced here: 33.8 us
  Pallas kernels  31.9 us (94%)
  between operations  0.66 us (2%)
  loops' own time  0.63 us (2%)
  local copies, waits for them, and re-layouts  0.61 us (2%)
    pallas_call x1, Pallas kernels, on_device(): lax.switch(mig_hop[0] - 1, [call(hop) for hop in range(1, 32)], block_tab...  31.9 us

profile of v2, /device:TPU:6, one launch (start us, length us, event | category | flops | bytes accessed | tf_op | source)
XLA Modules:
  0.0 33.8 jit_solution(5592664127205468747)
XLA Ops:
  0.7 32.5 %conditional.1 = (bf16[20,448]{1,0:T(8,128)(2,1)S(1)}) conditional(s32[]{:T(128)} %bitcast, (s32[1,16]{1,0:T(1,128)}, s32[4,32]{1,0:T(4,128)}, s32[32]{0:T(128)}, s32[32]{0:T(128)}, bf16[20,256]{1,0:T(8,128)(2,1)}, /*index=5*/bf16[20,2,128]{2,1,0:T(2,128)(2,1)}, bf16[2,16,128,128]{3,2,1,0:T(8,128)(2,1)}, ...), branch_computations={%region_0.0_spmd, %region_1.0_spmd, %region_2.0_spmd, %region_3.0_... | conditional | flops 58720256 | bytes 5242888 | solution.py:238
  0.9 31.9 %branch_15_fun.1 = bf16[20,448]{1,0:T(8,128)(2,1)S(1)} custom-call(s32[1,16]{1,0:T(1,128)} %get-tuple-element.983.table_hbm, s32[4,32]{1,0:T(4,128)} %get-tuple-element.654.lengths_hbm, s32[32]{0:T(128)} %get-tuple-element.1014.mig_slot_hbm, s32[32]{0:T(128)} %get-tuple-element.1045.handover_hbm, bf16[20,256]{1,0:T(8,128)(2,1)} %get-tuple-element.1076.q_hbm, ...), custom_call_target="tpu_custom_call" | custom-call | flops 58720256 | bytes 5242880 | tf_op jit(solution)/shard_map/cond/branch_15_fun/pallas_call | solution.py:238
  33.2 0.6 %copy.260 = bf16[20,448]{1,0:T(8,128)(2,1)} copy(bf16[20,448]{1,0:T(8,128)(2,1)S(1)} %get-tuple-element.781) | data formatting | bytes 35840
